TPU v7x, 512 devices: a whole 4x4x16 slice. The times are simulated.
512 devices in a mesh: grp: 16 (over z), tile: 8 (over x_hi, y), arch: 4 (over x_lo, core).
Axes of the slice: x: 4 (x_hi: 2, x_lo: 2; x = x_hi * 2 + x_lo), y: 4, z: 16, core: 2. Of those that a mesh axis runs over, the one named last changes fastest.
Arguments:
- query_grads: bfloat16 [4, 1536, 4096], P('arch', 'tile', 'grp'), may hold values from -6 to 6
- input_basis: bfloat16 [4096, 4096], P(None, 'grp'), may hold values from -0.09375 to 0.09375
- output_basis: bfloat16 [1536, 1536], P(None, 'tile'), may hold values from -0.15625 to 0.15625
- eigenvalues: float32 [1536, 4096], P('tile', 'grp'), may hold values from 0.1 to 10
- activations: bfloat16 [1024, 4096], P('arch', 'grp'), may hold values from -6 to 6
- gradients: bfloat16 [1024, 1536], P('arch', 'tile'), may hold values from -0.0099487305 to 0.0099487305
- seq_lengths: int32 [4, 8], P('arch'), may hold values from 1 to 128, 256 in all within a row
Outputs:
- preconditioned: bfloat16 [4, 4096, 1536], P('arch', 'grp', 'tile')
- sequence_scores: float32 [4, 32], P(None, 'arch')
Inputs may be any that keep to these rules, and one draw needn't show every extreme that they name: Each row of seq_lengths sums to 256, and its largest entry is exactly 128.
All inputs are finite; a program needn't handle non-finite values.
Results may differ from a plain program's by a relative error of at most 0.013.
Values may be sent and summed in bfloat16 or wider, within the bound.
A program may use at most 64 MiB of HBM per device.

v0:
```python
import jax
import jax.numpy as jnp
from jax import lax
from jax.sharding import PartitionSpec as P

damping = 0.01


def contract_first(left_side, right_side):
    return lax.dot_general(
        left_side, right_side, (((0,), (0,)), ((), ())), preferred_element_type=jnp.float32
    )


def contract_last(left_side, right_side):
    return lax.dot_general(
        left_side, right_side, (((1,), (1,)), ((), ())), preferred_element_type=jnp.float32
    )


def per_device(
    query_grads, input_basis, output_basis, eigenvalues, activations, gradients, seq_lengths
):
    local_query = query_grads[0]
    feat_rows = local_query.shape[0]
    input_cols = local_query.shape[1]
    basis_part = input_basis
    rotated_in = jnp.dot(
        lax.all_gather(local_query, "grp", axis=1, tiled=True),
        basis_part,
        preferred_element_type=jnp.float32,
    ).astype(jnp.bfloat16)
    basis_part = output_basis
    rotated = contract_first(basis_part, lax.all_gather(rotated_in, "tile", axis=0, tiled=True))
    scaled = (rotated / (eigenvalues + damping)).astype(jnp.bfloat16)
    basis_part = output_basis
    restored = lax.psum_scatter(
        jnp.dot(basis_part, scaled, preferred_element_type=jnp.float32).astype(jnp.bfloat16),
        "tile",
        scatter_dimension=0,
        tiled=True,
    )
    basis_part = input_basis
    summed = lax.psum_scatter(
        contract_last(basis_part, restored), "grp", scatter_dimension=0, tiled=True
    )
    preconditioned = summed.astype(jnp.bfloat16)
    all_queries = lax.all_gather(preconditioned[None], "arch", axis=0, tiled=True)
    query_count = all_queries.shape[0]
    stacked = jnp.transpose(all_queries, (1, 0, 2)).reshape(input_cols, query_count * feat_rows)
    projected = jnp.dot(activations, stacked, preferred_element_type=jnp.float32)
    projected = projected.reshape(activations.shape[0], query_count, feat_rows)
    partial_scores = jnp.sum(projected * gradients.astype(jnp.float32)[:, None, :], axis=2).T
    lengths = seq_lengths[0]
    ends = jnp.cumsum(lengths)
    starts = ends - lengths
    position = jnp.arange(activations.shape[0], dtype=jnp.int32)
    member = ((position[None, :] >= starts[:, None]) & (position[None, :] < ends[:, None])).astype(
        jnp.float32
    )
    seq_sizes = lengths.astype(jnp.float32)
    token_scores = lax.psum(partial_scores, ("grp", "tile"))
    totals = jnp.dot(token_scores, member.T, precision=lax.Precision.HIGHEST)
    sequence_scores = totals / seq_sizes[None, :]
    return (preconditioned[None], sequence_scores)


def solution(mesh):
    return jax.shard_map(
        per_device,
        mesh=mesh,
        in_specs=(
            P("arch", "tile", "grp"),
            P(None, "grp"),
            P(None, "tile"),
            P("tile", "grp"),
            P("arch", "grp"),
            P("arch", "tile"),
            P("arch", None),
        ),
        out_specs=(P("arch", "grp", "tile"), P(None, "arch")),
        check_vma=False,
    )
```

profile of v0, /device:TPU:2, one launch (start us, length us, event | category | flops | bytes accessed | tf_op | source)
XLA Modules:
  0.0 666.5 jit_solution(9814027762734079321)
XLA Ops:
  7.2 0.0 copy-start
  7.2 0.0 all-gather.4.cloned.1.call-start
  7.2 0.7 all-gather.4.cloned.1.call-update
  7.9 0.0 copy-start.1
  7.9 0.0 reduce-scatter.7.cloned.1.call-start
  8.0 82.4 %all-gather.4.cloned.1.call-done = bf16[1,192,4096]{2,1,0:T(8,128)(2,1)} async-done(((bf16[1,192,256]{2,1,0:T(8,128)(2,1)}), bf16[1,192,4096]{2,1,0:T(8,128)(2,1)}) %all-gather.4.cloned.1.call-update) | async-done | bytes 1572880 | tf_op jit(solution)/shard_map/all_gather | solution.py:29
  90.3 0.0 copy-done
  90.3 2.0 fusion.5
  92.3 35.8 %all_gather.10 = bf16[1536,256]{1,0:T(8,128)(2,1)S(1)} all-gather(bf16[192,256]{1,0:T(8,128)(2,1)S(1)} %fusion.5), channel_id=1, replica_groups=mesh['grp'=16,'tile'=8,'arch'=4] {'tile'}, dimensions={0}, use_global_device_ids=true | all-gather | bytes 884736 | tf_op jit(solution)/shard_map/all_gather | solution.py:34
  128.2 0.0 copy-done.1
  128.2 2.8 fusion
  131.0 2.3 copy.11
  133.3 0.0 reduce-scatter.7.cloned.1.call-update
  133.3 0.0 reduce-scatter.5.cloned.1.call-start
  133.3 81.0 %reduce-scatter.7.cloned.1.call-done = bf16[192,256]{1,0:T(8,128)(2,1)} async-done(((bf16[1536,256]{1,0:T(8,128)(2,1)}), bf16[192,256]{1,0:T(8,128)(2,1)}) %reduce-scatter.7.cloned.1.call-update) | async-done | bytes 98320
  214.3 3.4 convolution_bitcast_fusion
  217.7 0.0 copy-start.4
  217.7 0.0 copy-start.5
  217.7 0.0 reduce-scatter.5.cloned.1.call-update
  217.8 0.9 copy-done.4
  218.6 0.0 copy-done.5
  218.6 0.2 reduce-window.7
  218.8 75.6 %reduce-scatter.5.cloned.1.call-done = f32[256,192]{0,1:T(8,128)} async-done(((f32[4096,192]{0,1:T(8,128)}), f32[256,192]{0,1:T(8,128)}) %reduce-scatter.5.cloned.1.call-update) | async-done | bytes 196624 | tf_op jit(solution)/shard_map/reduce_scatter | solution.py:44
  294.4 1.0 convert_element_type.27
  295.4 6.1 all-gather.1
  301.6 0.0 copy-done.3
  301.6 0.3 fusion.15
  301.9 0.1 multiply_reduce_fusion
  302.0 356.6 %psum.7 = f32[4,256]{1,0:T(4,128)S(1)} all-reduce(f32[4,256]{1,0:T(4,128)S(1)} %bitcast.50), channel_id=1, replica_groups=mesh['grp'=16,'tile'=8,'arch'=4] {'grp','tile'}, use_global_device_ids=true, to_apply=%region_3.0 | all-reduce | flops 1024 | bytes 8192 | tf_op jit(solution)/shard_map/psum | solution.py:62
  658.6 0.8 convolution_divide_fusion
  659.4 0.0 copy-done.2
  659.4 0.7 convert_bitcast_fusion.1
  (6 shorter events, 0.1 us)
Async XLA Ops:
  7.2 83.2 %copy-start = (bf16[4096,256]{1,0:T(8,128)(2,1)S(1)}, bf16[4096,256]{1,0:T(8,128)(2,1)}, u32[]{:S(2)}) copy-start(bf16[4096,256]{1,0:T(8,128)(2,1)} %param.8) | copy-start | bytes 6291460
  7.2 83.2 %all-gather.4.cloned.1.call-start = ((), (), s32[]{:S(2)}) async-start(), calls=%async_computation.3 | async-start | bytes 1671168 | tf_op jit(solution)/shard_map/all_gather | solution.py:29
  7.9 120.3 %copy-start.1 = (bf16[1536,192]{0,1:T(8,128)(2,1)S(1)}, bf16[1536,192]{0,1:T(8,128)(2,1)}, u32[]{:S(2)}) copy-start(bf16[1536,192]{0,1:T(8,128)(2,1)} %param.9) | copy-start | bytes 1769476
  7.9 206.4 %reduce-scatter.7.cloned.1.call-start = ((), (), s32[]{:S(2)}) async-start(), calls=%async_computation.4 | async-start | bytes 884736
  133.3 161.1 %reduce-scatter.5.cloned.1.call-start = ((), (), s32[]{:S(2)}) async-start(), calls=%async_computation.2 | async-start | bytes 3342336 | tf_op jit(solution)/shard_map/reduce_scatter | solution.py:44
  217.7 0.9 copy-start.4
  217.7 0.9 copy-start.5
  217.7 83.9 %copy-start.3 = (bf16[256,256]{1,0:T(8,128)(2,1)S(1)}, bf16[256,256]{1,0:T(8,128)(2,1)}, u32[]{:S(2)}) copy-start(bf16[256,256]{1,0:T(8,128)(2,1)} %param.11) | copy-start | bytes 393220
  294.4 364.9 %copy-start.2 = (f32[256,192]{0,1:T(8,128)S(1)}, f32[256,192]{0,1:T(8,128)}, u32[]{:S(2)}) copy-start(f32[256,192]{0,1:T(8,128)} %reduce-scatter.5.cloned.1.call-done) | copy-start | bytes 589828
Sparse Core Ops, SparseCore 0:
  10.0 80.2 all-gather.3
  133.4 80.8 reduce-scatter.6
  217.9 76.5 reduce-scatter.4
where the time goes:
time: 667 us
  blocking collectives  399 us (60%)
  waiting for transfers between devices  240 us (36%)
  between operations  13.8 us (2%)
  matrix products  9.26 us (1%)
    psum x1, blocking collectives, per_device(): token_scores = lax.psum(partial_scores, ('grp', 'tile'))  357 us
    all_gather x1, waiting for transfers between devices, per_device(): lax.all_gather(local_query, 'grp', axis=1, tiled=True)  82.4 us
    unnamed x4, waiting for transfers between devices  81.7 us
    reduce_scatter x1, waiting for transfers between devices, per_device(): lax.psum_scatter(contract_last(basis_part, restored), 'grp', scatter_dime...  75.6 us
    all_gather x1, blocking collectives, per_device(): lax.all_gather(rotated_in, 'tile', axis=0, tiled=True)  35.8 us
  transfers between devices with their start and end apart: 3, of which 3 were waited for; matrix products, arithmetic and copies ran while one was open for 0% of the time, Pallas kernels for 0%

commit v1 on v0

--- a/solution.py
+++ b/solution.py
@@ -59,7 +59,7 @@
         jnp.float32
     )
     seq_sizes = lengths.astype(jnp.float32)
-    token_scores = lax.psum(partial_scores, ("grp", "tile"))
+    token_scores = lax.psum(lax.psum(partial_scores, "tile"), "grp")
     totals = jnp.dot(token_scores, member.T, precision=lax.Precision.HIGHEST)
     sequence_scores = totals / seq_sizes[None, :]
     return (preconditioned[None], sequence_scores)

time: 667 us -> 362 us (0.54)
  the two profiles are of different devices: /device:TPU:2 before, /device:TPU:32 now
where the time goes in v1:
time: 362 us
  waiting for transfers between devices  238 us (66%)
  blocking collectives  94.8 us (26%)
  between operations  13.8 us (4%)
  matrix products  9.28 us (3%)
    unnamed x4, waiting for transfers between devices  82.5 us
    all_gather x1, waiting for transfers between devices, per_device(): lax.all_gather(local_query, 'grp', axis=1, tiled=True)  81.7 us
    reduce_scatter x1, waiting for transfers between devices, per_device(): lax.psum_scatter(contract_last(basis_part, restored), 'grp', scatter_dime...  74.2 us
    psum x2, blocking collectives, per_device(): token_scores = lax.psum(lax.psum(partial_scores, 'tile'), 'grp')  52.1 us
    all_gather x1, blocking collectives, per_device(): lax.all_gather(rotated_in, 'tile', axis=0, tiled=True)  36 us
  transfers between devices with their start and end apart: 3, of which 3 were waited for; matrix products, arithmetic and copies ran while one was open for 0% of the time, Pallas kernels for 0%

profile of v1, /device:TPU:32, one launch (start us, length us, event | category | flops | bytes accessed | tf_op | source)
XLA Modules:
  0.0 361.5 jit_solution(6966764965037807962)
XLA Ops:
  7.2 0.0 copy-start
  7.2 0.0 all-gather.4.cloned.1.call-start
  7.2 0.7 all-gather.4.cloned.1.call-update
  7.9 0.0 copy-start.1
  7.9 0.0 reduce-scatter.7.cloned.1.call-start
  8.0 81.7 %all-gather.4.cloned.1.call-done = bf16[1,192,4096]{2,1,0:T(8,128)(2,1)} async-done(((bf16[1,192,256]{2,1,0:T(8,128)(2,1)}), bf16[1,192,4096]{2,1,0:T(8,128)(2,1)}) %all-gather.4.cloned.1.call-update) | async-done | bytes 1572880 | tf_op jit(solution)/shard_map/all_gather | solution.py:29
  89.7 0.0 copy-done
  89.7 2.0 fusion.5
  91.7 36.0 %all_gather.10 = bf16[1536,256]{1,0:T(8,128)(2,1)S(1)} all-gather(bf16[192,256]{1,0:T(8,128)(2,1)S(1)} %fusion.5), channel_id=1, replica_groups=mesh['grp'=16,'tile'=8,'arch'=4] {'tile'}, dimensions={0}, use_global_device_ids=true | all-gather | bytes 884736 | tf_op jit(solution)/shard_map/all_gather | solution.py:34
  127.7 0.0 copy-done.1
  127.7 2.8 fusion
  130.5 2.3 copy.11
  132.8 0.0 reduce-scatter.7.cloned.1.call-update
  132.8 0.0 reduce-scatter.5.cloned.1.call-start
  132.9 81.8 %reduce-scatter.7.cloned.1.call-done = bf16[192,256]{1,0:T(8,128)(2,1)} async-done(((bf16[1536,256]{1,0:T(8,128)(2,1)}), bf16[192,256]{1,0:T(8,128)(2,1)}) %reduce-scatter.7.cloned.1.call-update) | async-done | bytes 98320
  214.7 3.4 convolution_bitcast_fusion
  218.1 0.0 copy-start.4
  218.1 0.0 reduce-scatter.5.cloned.1.call-update
  218.1 0.9 copy-done.4
  219.0 0.0 copy-done.5
  219.0 0.2 reduce-window.7
  219.2 74.2 %reduce-scatter.5.cloned.1.call-done = f32[256,192]{0,1:T(8,128)} async-done(((f32[4096,192]{0,1:T(8,128)}), f32[256,192]{0,1:T(8,128)}) %reduce-scatter.5.cloned.1.call-update) | async-done | bytes 196624 | tf_op jit(solution)/shard_map/reduce_scatter | solution.py:44
  293.4 1.0 convert_element_type.27
  294.4 6.7 %all-gather.1 = bf16[1024,192]{0,1:T(8,128)(2,1)S(1)} all-gather(bf16[256,192]{0,1:T(8,128)(2,1)S(1)} %convert_element_type.27), channel_id=3, replica_groups=mesh['grp'=16,'tile'=8,'arch'=4] {'arch'}, dimensions={0}, use_global_device_ids=true | all-gather | bytes 491520 | tf_op jit(solution)/shard_map/all_gather | solution.py:48
  301.1 0.0 copy-done.3
  301.1 0.3 fusion.15
  301.4 0.1 multiply_reduce_fusion
  301.5 23.8 %psum.14 = f32[4,256]{1,0:T(4,128)S(1)} all-reduce(f32[4,256]{1,0:T(4,128)S(1)} %bitcast.50), channel_id=1, replica_groups=mesh['grp'=16,'tile'=8,'arch'=4] {'tile'}, use_global_device_ids=true, to_apply=%region_3.0 | all-reduce | flops 1024 | bytes 8192 | tf_op jit(solution)/shard_map/psum | solution.py:62
  325.3 28.3 %psum.15 = f32[4,256]{1,0:T(4,128)S(1)} all-reduce(f32[4,256]{1,0:T(4,128)S(1)} %psum.14), channel_id=1, replica_groups=mesh['grp'=16,'tile'=8,'arch'=4] {'grp'}, use_global_device_ids=true, to_apply=%region_4.5 | all-reduce | flops 1024 | bytes 8192 | tf_op jit(solution)/shard_map/psum | solution.py:62
  353.6 0.8 convolution_divide_fusion
  354.4 0.0 copy-done.2
  354.4 0.7 convert_bitcast_fusion.1
  (7 shorter events, 0.1 us)
Async XLA Ops:
  7.2 82.5 %copy-start = (bf16[4096,256]{1,0:T(8,128)(2,1)S(1)}, bf16[4096,256]{1,0:T(8,128)(2,1)}, u32[]{:S(2)}) copy-start(bf16[4096,256]{1,0:T(8,128)(2,1)} %param.8) | copy-start | bytes 6291460
  7.2 82.5 %all-gather.4.cloned.1.call-start = ((), (), s32[]{:S(2)}) async-start(), calls=%async_computation.3 | async-start | bytes 1671168 | tf_op jit(solution)/shard_map/all_gather | solution.py:29
  7.9 119.8 %copy-start.1 = (bf16[1536,192]{0,1:T(8,128)(2,1)S(1)}, bf16[1536,192]{0,1:T(8,128)(2,1)}, u32[]{:S(2)}) copy-start(bf16[1536,192]{0,1:T(8,128)(2,1)} %param.9) | copy-start | bytes 1769476
  7.9 206.8 %reduce-scatter.7.cloned.1.call-start = ((), (), s32[]{:S(2)}) async-start(), calls=%async_computation.4 | async-start | bytes 884736
  132.8 160.5 %reduce-scatter.5.cloned.1.call-start = ((), (), s32[]{:S(2)}) async-start(), calls=%async_computation.2 | async-start | bytes 3342336 | tf_op jit(solution)/shard_map/reduce_scatter | solution.py:44
  218.1 0.9 copy-start.4
  218.1 0.9 copy-start.5
  218.1 83.0 %copy-start.3 = (bf16[256,256]{1,0:T(8,128)(2,1)S(1)}, bf16[256,256]{1,0:T(8,128)(2,1)}, u32[]{:S(2)}) copy-start(bf16[256,256]{1,0:T(8,128)(2,1)} %param.11) | copy-start | bytes 393220
  293.4 61.0 %copy-start.2 = (f32[256,192]{0,1:T(8,128)S(1)}, f32[256,192]{0,1:T(8,128)}, u32[]{:S(2)}) copy-start(f32[256,192]{0,1:T(8,128)} %reduce-scatter.5.cloned.1.call-done) | copy-start | bytes 589828
Sparse Core Ops, SparseCore 0:
  10.0 79.6 all-gather.3
  133.0 81.6 reduce-scatter.6
  218.2 75.1 reduce-scatter.4
